TPU v7x, 256 devices: a whole 4x4x8 slice. The times are simulated.
256 devices in a mesh: dp: 16 (over y_hi, z), blk: 16 (over x, y_lo, core).
Axes of the slice: x: 4, y: 4 (y_hi: 2, y_lo: 2; y = y_hi * 2 + y_lo), z: 8, core: 2. Of those that a mesh axis runs over, the one named last changes fastest.
Arguments:
- images: bfloat16 [131072, 768], P(('dp', 'blk')), may hold values from -0.5412659 to 0.5412659
- captions: bfloat16 [65536, 768], P(('dp', 'blk')), may hold values from -0.5412659 to 0.5412659
- cap_target: int32 [16, 4096], P('dp'), may hold values from 0 to 8191
- cap_count: int32 [16, 256], P('dp'), may hold values from 6 to 16, as said below
Outputs:
- loss_value: float32 [], replicated
- grad_images: float32 [131072, 768], P(('dp', 'blk'))
- grad_captions: float32 [65536, 768], P(('dp', 'blk'))
Inputs may be any that keep to these rules, and one draw needn't show every extreme that they name: `cap_count`: entry [g, b * 16 + a] is how many leading slots, of the 16 that the device at dp index a and blk index b sends to data group g, hold a caption; the others are empty. In every draw one data group receives 16 filled slots from every dp index at one blk index.
All inputs are finite; a program needn't handle non-finite values.
Results may differ from a plain program's by a relative error of at most 0.0008.
Values may be sent and summed in bfloat16 or wider, within the bound.
No kernel may reach another device: no remote copies, remote signals or barrier semaphores. Data moves between devices by JAX's collectives and lax.ppermute only.
A program may use at most 128 MiB of HBM per device.

v0:
```python
import jax
import jax.numpy as jnp
from jax import lax
from jax.sharding import PartitionSpec as P

LOGIT_SCALE = 50.0
VERY_LOW = -1e30


def column_scores(images, texts_part):
    return (
        jnp.einsum("id,kd->ik", images, texts_part, preferred_element_type=jnp.float32)
        * LOGIT_SCALE
    )


def exact_rows(weights, embeds):
    return jnp.dot(weights, embeds.astype(jnp.float32), precision=lax.Precision.HIGHEST)


def exact_cols(weights, embeds):
    return jnp.einsum(
        "ik,id->kd", weights, embeds.astype(jnp.float32), precision=lax.Precision.HIGHEST
    )


def shards(images, captions, cap_target, cap_count):
    img_rows = images.shape[0]
    groups = lax.axis_size("dp")
    blocks = lax.axis_size("blk")
    received = lax.all_to_all(captions, "dp", split_axis=0, concat_axis=0, tiled=True)
    recv_rows = received.shape[0]
    slot_size = recv_rows // groups
    targets = cap_target[0]
    group_slots = targets.shape[0]
    live_all = (
        lax.iota(jnp.int32, group_slots) % slot_size < jnp.repeat(cap_count[0], slot_size)
    ).astype(jnp.float32)
    index_blk = lax.axis_index("blk")
    live_total = jnp.sum(live_all)
    group_images = img_rows * blocks
    balance = group_images / live_total
    image_ids = index_blk * img_rows + lax.iota(jnp.int32, img_rows)
    my_first = index_blk * recv_rows

    def slices():
        hit_mask = jnp.where(targets[None, :] == image_ids[:, None], live_all[None, :], 0.0)
        return (live_all, hit_mask)

    row_max = jnp.full((img_rows,), VERY_LOW, jnp.float32)
    scores = column_scores(images, lax.all_gather(received, "blk", axis=0, tiled=True))
    live_mask, hit_mask = slices()
    alive_mask = live_mask[None, :] > 0.0
    new_max = jnp.maximum(row_max, jnp.max(jnp.where(alive_mask, scores, VERY_LOW), axis=1))
    row_mass = jnp.sum(jnp.where(alive_mask, jnp.exp(scores - new_max[:, None]), 0.0), axis=1)
    row_sum = row_mass
    pos_sum = jnp.sum(hit_mask * scores, axis=1)
    pos_count = jnp.sum(hit_mask, axis=1)
    col_peak_part = jnp.max(scores, axis=0)
    col_mass_part = jnp.sum(jnp.exp(scores - col_peak_part[None, :]), axis=0)
    col_max = col_peak_part
    col_sum = col_mass_part
    totals = (new_max, row_sum, pos_sum, pos_count, col_max, col_sum)
    row_max, row_sum, pos_sum, pos_count, col_max, col_sum = totals
    peak_all = lax.pmax(col_max, "blk")
    mass_all = lax.psum(col_sum * jnp.exp(col_max - peak_all), "blk")
    col_lse = peak_all + jnp.log(mass_all)
    row_lse = row_max + jnp.log(row_sum)
    hit_floor = jnp.maximum(pos_count, 1.0)
    own_lse = lax.dynamic_slice_in_dim(live_all * col_lse, my_first, recv_rows)
    image_part = jnp.sum(row_lse - pos_sum / hit_floor) / group_images
    caption_part = (jnp.sum(own_lse) - jnp.sum(pos_sum)) / live_total
    loss_share = 0.5 * (image_part + caption_part) / groups
    texts_part = lax.all_gather(received, "blk", axis=0, tiled=True)
    scores = column_scores(images, texts_part)
    live_mask, hit_mask = slices()
    alive_mask = live_mask[None, :] > 0.0
    row_prob = jnp.where(alive_mask, jnp.exp(scores - row_lse[:, None]), 0.0)
    col_prob = jnp.where(alive_mask, jnp.exp(scores - col_lse[None, :]), 0.0)
    weights = 0.5 * (row_prob - hit_mask / hit_floor[:, None]) + 0.5 * balance * (
        col_prob - hit_mask
    )
    image_acc = exact_rows(weights, texts_part)
    text_term = exact_cols(weights, images)
    text_acc = text_term
    image_acc, text_acc = (image_acc, text_acc)
    image_grad = image_acc * LOGIT_SCALE
    text_grad = lax.psum_scatter(text_acc * LOGIT_SCALE, "blk", scatter_dimension=0, tiled=True)
    loss_value = lax.psum(loss_share, ("dp", "blk"))
    grad_captions = lax.all_to_all(text_grad, "dp", split_axis=0, concat_axis=0, tiled=True)
    return (loss_value, image_grad, grad_captions)


def solution(mesh):
    return jax.shard_map(
        shards,
        mesh=mesh,
        in_specs=(P(("dp", "blk"), None), P(("dp", "blk"), None), P("dp", None), P("dp", None)),
        out_specs=(P(), P(("dp", "blk"), None), P(("dp", "blk"), None)),
        check_vma=False,
    )
```

profile of v0, /device:TPU:1, one launch (start us, length us, event | category | flops | bytes accessed | tf_op | source)
XLA Modules:
  0.0 401.3 jit_solution(18221387807113736885)
XLA Ops:
  7.2 0.0 copy-start
  7.2 0.0 all-gather.2.cloned.1.call-start
  7.2 24.2 %all_to_all.24 = bf16[16,16,768]{2,1,0:T(8,128)(2,1)} all-to-all(bf16[16,16,768]{2,1,0:T(8,128)(2,1)} %bitcast.13), channel_id=1, replica_groups=mesh['dp'=16,'blk'=16] {'dp'}, dimensions={0} | all-to-all | bytes 786432 | tf_op jit(solution)/shard_map/all_to_all | solution.py:31
  31.5 0.0 all-gather.2.cloned.1.call-update
  31.5 0.0 reduce-scatter.2.cloned.1.call-start
  31.5 0.8 broadcast_in_dim.57
  32.3 0.1 reshape.54
  32.4 1.5 convert_reduce_fusion
  34.6 41.0 %all-gather.2.cloned.1.call-done = bf16[4096,768]{1,0:T(8,128)(2,1)} async-done(((bf16[256,768]{1,0:T(8,128)(2,1)}), bf16[4096,768]{1,0:T(8,128)(2,1)}) %all-gather.2.cloned.1.call-update) | async-done | bytes 6291472 | tf_op jit(solution)/shard_map/all_gather | solution.py:51
  75.7 0.0 copy-done
  75.7 0.0 copy-start.1
  75.7 8.6 %fusion.15 = (f32[4096]{0:T(1024)S(1)}, f32[512]{0:T(512)S(1)}, f32[512,4096]{1,0:T(8,128)}) fusion(pred[4096]{0:T(1024)(128)(4,1)S(1)} %get-tuple-element.12, bf16[512,768]{1,0:T(8,128)(2,1)S(1)} %copy-done, bf16[4096,768]{1,0:T(8,128)(2,1)} %all-gather.2.cloned.1.call-done), kind=kOutput, calls=%fused_computation.38 | convolution fusion | flops 3229609472 | bytes 15489024 | tf_op jit(solution)/shard_map/id,kd->ik/dot_general | solution.py:12
  84.3 51.3 %pmax.7 = f32[4096]{0:T(1024)S(1)} all-reduce(f32[4096]{0:T(1024)S(1)} %get-tuple-element.7), channel_id=1, replica_groups=mesh['dp'=16,'blk'=16] {'blk'}, use_global_device_ids=true, to_apply=%region_6.7 | all-reduce | flops 4096 | bytes 32768 | tf_op jit(solution)/shard_map/pmax | solution.py:65
  135.5 0.0 copy-done.1
  135.5 8.9 %fusion.4 = (f32[]{:T(128)}, f32[512]{0:T(512)S(1)}, f32[4096]{0:T(1024)S(1)}, f32[512]{0:T(512)S(1)}, f32[512]{0:T(512)S(1)}) fusion(f32[512,4096]{1,0:T(8,128)} %get-tuple-element.15, f32[4096]{0:T(1024)S(1)} %convert_element_type.15, s32[4096]{0:T(1024)S(1)} %bitcast.14, s32[512]{0:T(512)S(1)} %iota_add_fusion, f32[4096]{0:T(1024)S(1)} %get-tuple-element.7, ...), kind=kLoop, calls=%fused_computation.12 | loop fusion | flops 23063040 | bytes 8468484 | tf_op jit(solution)/shard_map/reduce_sum | solution.py:72
  144.4 53.1 %psum.14 = f32[4096]{0:T(1024)S(1)} all-reduce(f32[4096]{0:T(1024)S(1)} %exponential_multiply_fusion), channel_id=1, replica_groups=mesh['dp'=16,'blk'=16] {'blk'}, use_global_device_ids=true, to_apply=%region_8.9 | all-reduce | flops 4096 | bytes 32768 | tf_op jit(solution)/shard_map/psum | solution.py:66
  197.5 0.6 subtract_reduce_fusion
  198.1 19.9 %convolution_multiply_fusion = f32[4096,768]{1,0:T(8,128)} fusion(bf16[512,768]{1,0:T(8,128)(2,1)S(1)} %copy-done, f32[512,4096]{1,0:T(8,128)} %get-tuple-element.15, f32[4096]{0:T(1024)S(1)} %log_add_fusion, f32[]{:T(128)S(6)} %mul.55, f32[512]{0:T(512)S(1)} %get-tuple-element.14, f32[512]{0:T(512)S(1)} %get-tuple-element.11, ...), kind=kOutput, calls=%fused_computation.11 | convolution fusion | flops 19355664384 | bytes 21817348 | tf_op jit(solution)/shard_map/ik,id->kd/dot_general | solution.py:22
  218.0 0.0 reduce-scatter.2.cloned.1.call-update
  218.0 0.7 fusion.12
  221.4 88.8 %psum.15 = f32[]{:T(128)} all-reduce(f32[]{:T(128)S(6)} %div.26), channel_id=1, replica_groups=mesh['dp'=16,'blk'=16] {'dp','blk'}, use_global_device_ids=true, to_apply=%region_12.13 | all-reduce | flops 1 | bytes 8 | tf_op jit(solution)/shard_map/psum | solution.py:89
  310.2 53.4 %reduce-scatter.2.cloned.1.call-done = f32[256,768]{1,0:T(8,128)} async-done(((f32[4096,768]{1,0:T(8,128)}), f32[256,768]{1,0:T(8,128)}) %reduce-scatter.2.cloned.1.call-update) | async-done | bytes 786448 | tf_op jit(solution)/shard_map/reduce_scatter | solution.py:88
  363.5 8.1 %all-to-all-start.1 = ((f32[16,16,768]{2,1,0:T(8,128)}), f32[16,16,768]{2,1,0:T(8,128)S(1)}, u32[]{:S(2)}, u32[]{:S(2)}) async-start(f32[16,16,768]{2,1,0:T(8,128)} %bitcast.12), calls=%async_computation.2 | async-start | bytes 1572864 | tf_op jit(solution)/shard_map/all_to_all | solution.py:90
  371.6 19.8 %convolution_multiply_fusion.2 = f32[512,768]{1,0:T(8,128)} fusion(bf16[4096,768]{1,0:T(8,128)(2,1)} %all-gather.2.cloned.1.call-done, f32[512,4096]{1,0:T(8,128)} %get-tuple-element.15, f32[4096]{0:T(1024)S(1)} %log_add_fusion, f32[]{:T(128)S(6)} %mul.55, f32[512]{0:T(512)S(1)} %get-tuple-element.14, f32[512]{0:T(512)S(1)} %get-tuple-element.11, ...), kind=kOutput, calls=%fused_computation.15 | convolution fusion | flops 19352911872 | bytes 16312324 | tf_op jit(solution)/shard_map/dot_general | solution.py:18
  391.4 2.1 all-to-all-done.1
  393.6 0.9 copy.8
  (6 shorter events, 0.0 us)
Async XLA Ops:
  7.2 68.5 %copy-start = (bf16[512,768]{1,0:T(8,128)(2,1)S(1)}, bf16[512,768]{1,0:T(8,128)(2,1)}, u32[]{:S(2)}) copy-start(bf16[512,768]{1,0:T(8,128)(2,1)} %param.4) | copy-start | bytes 2359300
  7.2 68.5 %all-gather.2.cloned.1.call-start = ((), (), s32[]{:S(2)}) async-start(), calls=%async_computation.3 | async-start | bytes 6684672 | tf_op jit(solution)/shard_map/all_gather | solution.py:51
  31.5 332.1 %reduce-scatter.2.cloned.1.call-start = ((), (), s32[]{:S(2)}) async-start(), calls=%async_computation.4 | async-start | bytes 13369344 | tf_op jit(solution)/shard_map/reduce_scatter | solution.py:88
  75.7 59.9 %copy-start.1 = (s32[1,4096]{1,0:T(1,128)S(1)}, s32[1,4096]{1,0:T(1,128)}, u32[]{:S(2)}) copy-start(s32[1,4096]{1,0:T(1,128)} %param.6) | copy-start | bytes 49156
  363.5 30.0 %all-to-all-start.1 = ((f32[16,16,768]{2,1,0:T(8,128)}), f32[16,16,768]{2,1,0:T(8,128)S(1)}, u32[]{:S(2)}, u32[]{:S(2)}) async-start(f32[16,16,768]{2,1,0:T(8,128)} %bitcast.12), calls=%async_computation.2 | async-start | bytes 1572864 | tf_op jit(solution)/shard_map/all_to_all | solution.py:90
Sparse Core Ops, SparseCore 0:
  31.6 44.0 all-gather.1
  218.1 145.3 reduce-scatter.1
where the time goes:
time: 402 us; the launch traced here: 401 us
  blocking collectives  217 us (54%)
  waiting for transfers between devices  96.6 us (24%)
  matrix products  48.3 us (12%)
  between operations  17.5 us (4%)
  other arithmetic  11.7 us (3%)
  starting transfers between devices  8.15 us (2%)
    psum x1, blocking collectives, shards(): loss_value = lax.psum(loss_share, ('dp', 'blk'))  88.8 us
    reduce_scatter x1, waiting for transfers between devices, shards(): lax.psum_scatter(text_acc * LOGIT_SCALE, 'blk', scatter_dimension=0, tile...  53.4 us
    psum x1, blocking collectives, shards(): mass_all = lax.psum(col_sum * jnp.exp(col_max - peak_all), 'blk')  53.1 us
    pmax x1, blocking collectives, shards(): peak_all = lax.pmax(col_max, 'blk')  51.3 us
    all_gather x1, waiting for transfers between devices, shards(): lax.all_gather(received, 'blk', axis=0, tiled=True)  41 us
    all_to_all x1, blocking collectives, shards(): lax.all_to_all(captions, 'dp', split_axis=0, concat_axis=0, tiled=True)  24.2 us
    dot_general x1, matrix products, exact_cols(): jnp.einsum('ik,id->kd', weights, embeds.astype(jnp.float32), precision=la...  19.9 us
    dot_general x1, matrix products, exact_rows(): jnp.dot(weights, embeds.astype(jnp.float32), precision=lax.Precision.HIGH...  19.8 us
  transfers between devices with their start and end apart: 3, of which 3 were waited for; matrix products, arithmetic and copies ran while one was open for 6% of the time, Pallas kernels for 0%

commit v1 on v0

v1 whole, which is shorter than its diff:
```python
import math

import jax
import jax.numpy as jnp
from jax import lax
from jax.experimental import pallas as pl
from jax.experimental.pallas import tpu as pltpu
from jax.sharding import PartitionSpec as P

LOGIT_SCALE = 50.0
SCALE_LOG2 = LOGIT_SCALE * math.log2(math.e)
LN2 = math.log(2.0)
VERY_LOW = -1e30
VERY_HIGH = 3e38
VMEM_BYTES = 56 * 1024 * 1024
F32 = jnp.float32
BF16 = jnp.bfloat16

XS, YS, CORES = 4, 2, 2
IMG = 512
CAP = 256
WIDTH = 768
ROWS = 4 * IMG
STEP = 256
STEPS = ROWS // STEP
PER = IMG // STEP


def params(**kw):
    return pltpu.CompilerParams(vmem_limit_bytes=VMEM_BYTES, **kw)


def whole(shape):
    return pl.BlockSpec(shape, lambda *_: (0,) * len(shape))


def image_part(j):
    return pl.BlockSpec((STEP, WIDTH), lambda i: (jnp.clip(i - PER * j, 0, PER - 1), 0))


def move(value, there):
    spots = [(x, y, c) for x in range(XS) for y in range(YS) for c in range(CORES)]
    flat = lambda x, y, c: (x * YS + y) * CORES + c
    return lax.ppermute(value, "blk", [(flat(*s), flat(*there(*s))) for s in spots])


def along_x(value, shift):
    return move(value, lambda x, y, c: ((x + shift) % XS, y, c))


def across(value, q):
    return move(value, lambda x, y, c: (x, y ^ (q >> 1), c ^ (q & 1)))


def row_of(column, lanes=128):
    return jnp.broadcast_to(column, (column.shape[0], lanes)).T[0:1, :]


def column_of(row, lanes=128):
    return jnp.broadcast_to(row, (lanes, row.shape[1])).T


def wide(column, lanes):
    return jnp.concatenate([column] * (lanes // column.shape[1]), axis=1)


def count_kernel(base_ref, balance_ref, targets_ref, out_ref):
    for step in range(STEPS):
        ids = (
            lax.broadcasted_iota(jnp.int32, (STEP, 128), 0)
            + (step % PER) * STEP
            + base_ref[step // PER]
        )

        def add(r, acc):
            return acc + jnp.where(targets_ref[pl.ds(r, 1), :] == ids, 1.0, 0.0)

        hits = lax.fori_loop(0, targets_ref.shape[0], add, jnp.zeros((STEP, 128), F32), unroll=4)
        count = jnp.sum(hits, axis=1, keepdims=True)
        weight = 0.5 / jnp.maximum(count, 1.0) + balance_ref[0]
        out_ref[pl.ds(step * STEP, STEP), :] = jnp.broadcast_to(weight, (STEP, 128))


def hit_weights(base, half_balance, targets):
    smem = pl.BlockSpec(memory_space=pltpu.SMEM)
    return pl.pallas_call(
        count_kernel,
        out_shape=jax.ShapeDtypeStruct((ROWS, 128), F32),
        in_specs=[smem, smem, pl.BlockSpec(memory_space=pltpu.VMEM)],
        out_specs=pl.BlockSpec(memory_space=pltpu.VMEM),
        compiler_params=params(),
        cost_estimate=pl.CostEstimate(flops=20_000_000, bytes_accessed=1 << 20, transcendentals=0),
    )(base, half_balance, targets)


def hit_mask(targets_ref, j, d, step_row, rows):
    ids = lax.broadcasted_iota(jnp.int32, (rows, CAP), 0) + step_row
    return targets_ref[pl.ds(j * 4 + d, 1), :] == ids


def scores_kernel(
    x0, x1, x2, x3, t0, t1, t2, t3, cap_ref, targets_ref, weight_ref,
    s_ref, row_ref, col_ref, xs, cm, cs, hs,
):
    i = pl.program_id(0)
    j = i // PER
    for n, ref in enumerate((x0, x1, x2, x3)):

        @pl.when(j == n)
        def _():
            xs[...] = ref[...]

    @pl.when(i == 0)
    def _():
        cm[...] = jnp.full_like(cm, -VERY_HIGH)
        cs[...] = jnp.zeros_like(cs)
        hs[...] = jnp.zeros_like(hs)

    x = xs[...]
    weight = wide(weight_ref[...], CAP)
    peak = None
    hits = None
    for d, t in enumerate((t0, t1, t2, t3)):
        s = lax.dot_general(x, t[...], (((1,), (1,)), ((), ())), preferred_element_type=F32)
        s = jnp.minimum(s * SCALE_LOG2, cap_ref[d : d + 1, :])
        s_ref[d] = s
        peak = s if peak is None else jnp.maximum(peak, s)
        hit = jnp.where(hit_mask(targets_ref, j, d, (i % PER) * STEP, STEP), s * weight, 0.0)
        hits = hit if hits is None else hits + hit
        old = cm[d : d + 1, :]
        new = jnp.maximum(old, jnp.max(s, axis=0, keepdims=True))
        cm[d : d + 1, :] = new
        cs[d : d + 1, :] = cs[d : d + 1, :] * jnp.exp2(old - new) + jnp.sum(
            jnp.exp2(s - new), axis=0, keepdims=True
        )
    hs[0:1, :] = hs[0:1, :] + jnp.sum(hits, axis=0, keepdims=True)
    peak = jnp.max(peak, axis=1, keepdims=True)
    mass = None
    for d in range(4):
        e = jnp.exp2(s_ref[d] - peak)
        mass = e if mass is None else mass + e
    mass = jnp.sum(mass, axis=1, keepdims=True)
    row_ref[pl.ds(i, 1), :] = row_of(peak + jnp.log2(mass))

    @pl.when(i == STEPS - 1)
    def _():
        col_ref[0:4, :] = cm[0:4, :] + jnp.log2(cs[0:4, :])
        col_ref[4:8, :] = jnp.concatenate([hs[0:1, :], jnp.zeros((3, CAP), F32)], axis=0)


def scores(images, texts, cap, targets, weight):
    return pl.pallas_call(
        scores_kernel,
        grid=(STEPS,),
        out_shape=(
            jax.ShapeDtypeStruct((4, ROWS, CAP), F32),
            jax.ShapeDtypeStruct((STEPS, STEP), F32),
            jax.ShapeDtypeStruct((8, CAP), F32),
        ),
        in_specs=[image_part(j) for j in range(4)]
        + [whole((CAP, WIDTH))] * 4
        + [whole((8, CAP)), whole((16, CAP)), pl.BlockSpec((STEP, 128), lambda i: (i, 0))],
        out_specs=(
            pl.BlockSpec((4, STEP, CAP), lambda i: (0, i, 0)),
            whole((STEPS, STEP)),
            whole((8, CAP)),
        ),
        scratch_shapes=[
            pltpu.VMEM((STEP, WIDTH), BF16),
            pltpu.VMEM((8, CAP), F32),
            pltpu.VMEM((8, CAP), F32),
            pltpu.VMEM((8, CAP), F32),
        ],
        compiler_params=params(),
        cost_estimate=pl.CostEstimate(
            flops=2 * ROWS * 4 * CAP * WIDTH, bytes_accessed=14 << 20, transcendentals=4 << 20
        ),
    )(*images, *texts, cap, targets, weight)


def combine(parts):
    peak = parts[0]
    for p in parts[1:]:
        peak = jnp.maximum(peak, p)
    mass = None
    for p in parts:
        e = jnp.exp2(p - peak)
        mass = e if mass is None else mass + e
    return peak + jnp.log2(mass)


def pick(ref, order):
    return jnp.concatenate([ref[o : o + 1, :] for o in order], axis=0)


def two_terms(w):
    high = w.astype(BF16)
    return high, (w - high.astype(F32)).astype(BF16)


def text_kernel(
    scal_ref, s_ref, x0, x1, x2, x3, row0, row1, row2, row3, col0, col1, col2, col3,
    cap_ref, targets_ref, weight_ref,
    o0, o1, o2, o3, r_ref, c_ref, loss_ref, hi, lo,
):
    d = pl.program_id(0)

    @pl.when(d == 0)
    def _():
        rows = [
            pick(ref, [((i // PER) ^ q) * PER + i % PER for i in range(STEPS)])
            for q, ref in enumerate((row0, row1, row2, row3))
        ]
        r = combine(rows)
        cols = [
            pick(ref, [(n + e) % 4 for n in range(4)])
            for e, ref in enumerate((col0, col1, col2, col3))
        ]
        alive = cap_ref[0:4, :] > 0.0
        c = jnp.where(alive, combine(cols), 0.0)
        share = (
            jnp.sum(r) * scal_ref[1] + jnp.sum(c) * scal_ref[2] - jnp.sum(col0[4:5, :]) * scal_ref[3]
        )
        loss_ref[...] = jnp.full_like(loss_ref, share)
        c_ref[0:4, :] = jnp.where(alive, c - scal_ref[0], 0.0)
        c_ref[4:8, :] = jnp.zeros((4, CAP), F32)
        for i in range(STEPS):
            r_ref[i * STEP : (i + 1) * STEP, :] = column_of(r[i : i + 1, :] + 1.0)

    col = c_ref[pl.ds(d, 1), :]
    acc = None
    for j, x in enumerate((x0, x1, x2, x3)):
        for h in range(PER):
            at = slice((j * PER + h) * STEP, (j * PER + h + 1) * STEP)
            s = s_ref[0, at, :]
            w = jnp.exp2(s - wide(r_ref[at, :], CAP)) + jnp.exp2(s - col)
            w = w - jnp.where(
                hit_mask(targets_ref, j, d, h * STEP, STEP), wide(weight_ref[at, :], CAP), 0.0
            )
            hi[at, :], lo[at, :] = two_terms(w)
        at = slice(j * IMG, (j + 1) * IMG)
        for part in (hi, lo):
            term = lax.dot_general(
                part[at, :], x[...], (((0,), (0,)), ((), ())), preferred_element_type=F32
            )
            acc = term if acc is None else acc + term
    for n, o in enumerate((o0, o1, o2, o3)):

        @pl.when(d == n)
        def _():
            o[...] = acc


def text_terms(scal, s, images, rows, cols, cap, targets, weight):
    small = whole((8, CAP))
    return pl.pallas_call(
        text_kernel,
        grid=(4,),
        out_shape=(jax.ShapeDtypeStruct((CAP, WIDTH), F32),) * 4
        + (
            jax.ShapeDtypeStruct((ROWS, 128), F32),
            jax.ShapeDtypeStruct((8, CAP), F32),
            jax.ShapeDtypeStruct((8, 128), F32),
        ),
        in_specs=[
            pl.BlockSpec(memory_space=pltpu.SMEM),
            pl.BlockSpec((1, ROWS, CAP), lambda d: (d, 0, 0)),
        ]
        + [whole((IMG, WIDTH))] * 4
        + [small] * 9
        + [whole((16, CAP)), whole((ROWS, 128))],
        out_specs=(whole((CAP, WIDTH)),) * 4
        + (whole((ROWS, 128)), whole((8, CAP)), whole((8, 128))),
        scratch_shapes=[pltpu.VMEM((ROWS, CAP), BF16), pltpu.VMEM((ROWS, CAP), BF16)],
        compiler_params=params(),
        cost_estimate=pl.CostEstimate(
            flops=4 * ROWS * 4 * CAP * WIDTH, bytes_accessed=16 << 20, transcendentals=4 << 20
        ),
    )(scal, s, *images, *rows, *cols, cap, targets, weight)


def image_kernel(
    s_ref, r_ref, c_ref, t0, t1, t2, t3, targets_ref, weight_ref, y0, y1, y2, y3
):
    i = pl.program_id(0)
    j = i // PER
    acc = None
    r = wide(r_ref[...], CAP)
    weight = wide(weight_ref[...], CAP)
    for d, t in enumerate((t0, t1, t2, t3)):
        s = s_ref[d]
        w = jnp.exp2(s - r) + jnp.exp2(s - c_ref[d : d + 1, :])
        w = w - jnp.where(hit_mask(targets_ref, j, d, (i % PER) * STEP, STEP), weight, 0.0)
        for part in two_terms(w):
            term = jnp.dot(part, t[...], preferred_element_type=F32)
            acc = term if acc is None else acc + term
    for n, y in enumerate((y0, y1, y2, y3)):

        @pl.when(j == n)
        def _():
            y[...] = acc


def image_terms(s, r, c, texts, targets, weight):
    run = pl.BlockSpec((STEP, 128), lambda i: (i, 0))
    return pl.pallas_call(
        image_kernel,
        grid=(STEPS,),
        out_shape=(jax.ShapeDtypeStruct((IMG, WIDTH), F32),) * 4,
        in_specs=[pl.BlockSpec((4, STEP, CAP), lambda i: (0, i, 0)), run, whole((8, CAP))]
        + [whole((CAP, WIDTH))] * 4
        + [whole((16, CAP)), run],
        out_specs=tuple(image_part(j) for j in range(4)),
        compiler_params=params(),
        cost_estimate=pl.CostEstimate(
            flops=4 * ROWS * 4 * CAP * WIDTH, bytes_accessed=16 << 20, transcendentals=4 << 20
        ),
    )(s, r, c, *texts, targets, weight)


def total(value):
    value = sum((across(value, q) for q in (1, 2, 3)), value)
    value = sum((along_x(value, e) for e in (1, 2, 3)), value)
    n = lax.axis_size("dp")
    for unit in (1, 4):
        shifts = [(lambda a, e=e: a // (4 * unit) * (4 * unit) + (a + e * unit) % (4 * unit)) for e in (1, 2, 3)]
        value = sum((lax.ppermute(value, "dp", [(a, to(a)) for a in range(n)]) for to in shifts), value)
    return value


def shards(images, captions, cap_target, cap_count):
    groups = lax.axis_size("dp")
    blocks = lax.axis_size("blk")
    slots = cap_target.shape[1]
    slot_size = slots // (groups * blocks)
    me = lax.axis_index("blk")
    my_x, my_yc = me // (YS * CORES), me % (YS * CORES)

    image1 = across(images, 1)
    image2 = across(images, 2)
    received = lax.all_to_all(captions, "dp", split_axis=0, concat_axis=0, tiled=True)
    image3 = across(image2, 1)
    parts = (images, image1, image2, image3)
    texts = (received,) + tuple(along_x(received, -d) for d in (1, 2, 3))

    alive = lax.iota(jnp.int32, slots) % slot_size < jnp.repeat(cap_count[0], slot_size)
    targets = jnp.where(alive, cap_target[0], -1)
    caps = jnp.where(alive, VERY_HIGH, VERY_LOW).astype(F32)
    live = jnp.sum(cap_count[0]).astype(F32)
    group_images = float(IMG * blocks)
    half_balance = 0.5 * group_images / live
    order = [(my_x + d) % XS * (YS * CORES) + my_yc for d in range(4)]
    take = lambda a: jnp.stack([lax.dynamic_index_in_dim(a.reshape(blocks, CAP), o, 0, False) for o in order])
    base = jnp.stack([(my_x * 4 + (my_yc ^ q)) * IMG for q in range(4)]).astype(jnp.int32)
    my_targets = (take(targets)[None] - base[:, None, None]).reshape(16, CAP)
    my_caps = jnp.concatenate([take(caps), jnp.zeros((4, CAP), F32)], axis=0)
    weight = hit_weights(base, half_balance[None], targets.reshape(-1, 128))

    s, row, col = scores(parts, texts, my_caps, my_targets, weight)
    rows = (row,) + tuple(across(row, q) for q in (1, 2, 3))
    cols = (col,) + tuple(along_x(col, e) for e in (1, 2, 3))
    scal = jnp.stack(
        [
            jnp.log2(half_balance),
            jnp.float32(LN2 * 0.5 / group_images / 4 / groups),
            LN2 * 0.5 / live / 4 / groups,
            jnp.float32(LN2 / group_images / groups),
        ]
    )
    *terms, r, c, loss = text_terms(scal, s, parts, rows, cols, my_caps, my_targets, weight)
    sent = [along_x(terms[d], d) for d in (1, 2, 3)]
    y0, y1, y2, y3 = image_terms(s, r, c, texts, my_targets, weight)
    text_grad = (terms[0] + sent[0] + sent[1] + sent[2]) * LOGIT_SCALE
    grad_captions = lax.all_to_all(text_grad, "dp", split_axis=0, concat_axis=0, tiled=True)
    a3 = across(y3, 1)
    a1 = across(y1, 1)
    b = across(y2 + a3, 2)
    image_grad = (y0 + a1 + b) * LOGIT_SCALE
    loss_value = total(loss)[0, 0]
    return loss_value, image_grad, grad_captions


def solution(mesh):
    return jax.shard_map(
        shards,
        mesh=mesh,
        in_specs=(P(("dp", "blk"), None), P(("dp", "blk"), None), P("dp", None), P("dp", None)),
        out_specs=(P(), P(("dp", "blk"), None), P(("dp", "blk"), None)),
        check_vma=False,
    )
```

time: 402 us -> 194 us (0.48)
  blocking collectives: 217 us -> 0 us
  starting transfers between devices: 8.15 us -> 64.4 us
  matrix products: 48.3 us -> 0 us
  Pallas kernels: 0 us -> 48.3 us
  waiting for transfers between devices: 96.6 us -> 57.7 us
  between operations: 17.5 us -> 1.88 us
  local copies, waits for them, and re-layouts: 1.76 us -> 6.11 us
    psum x2 -> x0, blocking collectives: 142 us -> none  [the longest x1 88.8 us: shards(): loss_value = lax.psum(loss_share, ('dp', 'blk'))]
    ppermute x0 -> x30, waiting for transfers between devices: none -> 55.6 us  [the longest x24 50.4 us: move(): lax.ppermute(value, 'blk', [(flat(*s), flat(*there(*s))) for s in spots])]
    reduce_scatter x1 -> x0, waiting for transfers between devices: 53.4 us -> none  [shards(): lax.psum_scatter(text_acc * LOGIT_SCALE, 'blk', scatter_dimension=0, tile...]
    pmax x1 -> x0, blocking collectives: 51.3 us -> none  [shards(): peak_all = lax.pmax(col_max, 'blk')]
    pallas_call x0 -> x4, Pallas kernels: none -> 48.3 us  [the longest x1 14.3 us: text_terms(): pl.pallas_call(text_kernel, grid=(4,), out_shape=(jax.ShapeDtypeStruct((C...]
    dot_general x3 -> x0, matrix products: 48.3 us -> none  [the longest x1 19.9 us: exact_cols(): jnp.einsum('ik,id->kd', weights, embeds.astype(jnp.float32), precision=la...]
    ppermute x0 -> x30, starting transfers between devices: none -> 44.4 us  [the longest x24 28.7 us: move(): lax.ppermute(value, 'blk', [(flat(*s), flat(*there(*s))) for s in spots])]
    all_gather x1 -> x0, waiting for transfers between devices: 41 us -> none  [shards(): lax.all_gather(received, 'blk', axis=0, tiled=True)]
  transfers between devices with their start and end apart: 3 -> 32, of which waited for: 3 -> 15; matrix products, arithmetic and copies ran while one was open for 6% -> 6% of each run, Pallas kernels for 0% -> 4%
where the time goes in v1:
time: 194 us; the launch traced here: 191 us
  starting transfers between devices  64.4 us (33%)
  waiting for transfers between devices  57.7 us (30%)
  Pallas kernels  48.3 us (25%)
  other arithmetic  12.7 us (7%)
  local copies, waits for them, and re-layouts  6.11 us (3%)
    ppermute x24, waiting for transfers between devices, move(): lax.ppermute(value, 'blk', [(flat(*s), flat(*there(*s))) for s in spots])  50.4 us
    ppermute x24, starting transfers between devices, move(): lax.ppermute(value, 'blk', [(flat(*s), flat(*there(*s))) for s in spots])  28.7 us
    ppermute x6, starting transfers between devices, total(): lax.ppermute(value, 'dp', [(a, to(a)) for a in range(n)])  15.7 us
    pallas_call x1, Pallas kernels, text_terms(): pl.pallas_call(text_kernel, grid=(4,), out_shape=(jax.ShapeDtypeStruct((C...  14.3 us
    pallas_call x1, Pallas kernels, image_terms(): pl.pallas_call(image_kernel, grid=(STEPS,), out_shape=(jax.ShapeDtypeStru...  14.1 us
    pallas_call x1, Pallas kernels, scores(): pl.pallas_call(scores_kernel, grid=(STEPS,), out_shape=(jax.ShapeDtypeStr...  12.9 us
    all_to_all x1, starting transfers between devices, shards(): lax.all_to_all(captions, 'dp', split_axis=0, concat_axis=0, tiled=True)  10.4 us
    all_to_all x1, starting transfers between devices, shards(): lax.all_to_all(text_grad, 'dp', split_axis=0, concat_axis=0, tiled=True)  9.65 us
  transfers between devices with their start and end apart: 32, of which 15 were waited for; matrix products, arithmetic and copies ran while one was open for 6% of the time, Pallas kernels for 4%

profile of v1, /device:TPU:1, one launch (start us, length us, event | category | flops | bytes accessed | tf_op | source)
XLA Modules:
  0.0 191.1 jit_solution(14022354933419731932)
XLA Ops:
  0.6 2.2 %collective-permute-start.1 = (bf16[512,768]{1,0:T(8,128)(2,1)}, bf16[512,768]{1,0:T(8,128)(2,1)S(1)}, u32[]{:S(2)}, u32[]{:S(2)}) collective-permute-start(bf16[512,768]{1,0:T(8,128)(2,1)} %x0.3), channel_id=1, source_target_pairs={{0,2},{1,3},{2,0},{3,1},{4,6},{5,7},{6,4},{7,5},{8,10},{9,11},{10,... | collective-permute-start | bytes 2359304 | tf_op jit(solution)/shard_map/ppermute | solution.py:44
  4.1 10.4 %all-to-all-start = ((bf16[16,16,768]{2,1,0:T(8,128)(2,1)}), bf16[16,16,768]{2,1,0:T(8,128)(2,1)S(1)}, u32[]{:S(2)}, u32[]{:S(2)}) async-start(bf16[16,16,768]{2,1,0:T(8,128)(2,1)} %bitcast.16), calls=%async_computation | async-start | bytes 786432 | tf_op jit(solution)/shard_map/all_to_all | solution.py:341
  15.0 2.0 %fusion.5 = (s32[256]{0:T(256)S(1)}, s32[]{:T(128)}) fusion(s32[1,256]{1,0:T(1,128)} %param.7, s32[]{:T(128)} %broadcast.58), kind=kLoop, calls=%fused_computation.31 | loop fusion | flops 255 | bytes 2056 | tf_op args[3]
  17.2 1.4 reduce.10
  20.7 4.2 %collective-permute-start.2 = (bf16[512,768]{1,0:T(8,128)(2,1)S(1)}, bf16[512,768]{1,0:T(8,128)(2,1)S(1)}, u32[]{:S(2)}, u32[]{:S(2)}) collective-permute-start(bf16[512,768]{1,0:T(8,128)(2,1)S(1)} %collective-permute-done.1.x2), channel_id=1, source_target_pairs={{0,1},{1,0},{2,3},{3,2},{4,5},{5,4},{6,7},{7,6},{8,9},{9,8},{10,11... | collective-permute-start | bytes 2359304 | tf_op jit(solution)/shard_map/ppermute | solution.py:44
  25.6 2.1 %all-to-all-done = bf16[16,16,768]{2,1,0:T(8,128)(2,1)S(1)} async-done(((bf16[16,16,768]{2,1,0:T(8,128)(2,1)}), bf16[16,16,768]{2,1,0:T(8,128)(2,1)S(1)}, u32[]{:S(2)}, u32[]{:S(2)}) %all-to-all-start) | async-done | bytes 393248 | tf_op jit(solution)/shard_map/all_to_all | solution.py:341
  27.7 2.5 %collective-permute-start.3 = (bf16[256,768]{1,0:T(8,128)(2,1)S(1)}, bf16[256,768]{1,0:T(8,128)(2,1)S(1)}, u32[]{:S(2)}, u32[]{:S(2)}) collective-permute-start(bf16[256,768]{1,0:T(8,128)(2,1)S(1)} %bitcast.17), channel_id=1, source_target_pairs={{0,12},{1,13},{2,14},{3,15},{4,0},{5,1},{6,2},{7,3},{8,4},{9,5},{1... | collective-permute-start | bytes 1179656 | tf_op jit(solution)/shard_map/ppermute | solution.py:44
  32.0 6.9 %shard_map.67.weight_ref = f32[2048,128]{1,0:T(8,128)} custom-call(s32[4]{0:T(128)} %copy-done.4, f32[1]{0:T(128)} %bitcast.8.balance_ref, s32[32,128]{1,0:T(8,128)} %fusion.4.targets_ref), custom_call_target="tpu_custom_call" | custom-call | flops 20000000 | bytes 1048576 | tf_op jit(solution)/shard_map/pallas_call | solution.py:86
  40.1 11.1 %collective-permute-done.5.t3 = bf16[256,768]{1,0:T(8,128)(2,1)S(1)} collective-permute-done((bf16[256,768]{1,0:T(8,128)(2,1)S(1)}, bf16[256,768]{1,0:T(8,128)(2,1)S(1)}, u32[]{:S(2)}, u32[]{:S(2)}) %collective-permute-start.5) | collective-permute-done | bytes 393248 | tf_op jit(solution)/shard_map/ppermute | solution.py:44
  52.8 12.9 %shard_map.68 = (f32[4,2048,256]{2,1,0:T(8,128)}, f32[8,256]{1,0:T(8,128)}, f32[8,256]{1,0:T(8,128)}) custom-call(bf16[512,768]{1,0:T(8,128)(2,1)} %x0.3, bf16[512,768]{1,0:T(8,128)(2,1)} %copy-done.7, bf16[512,768]{1,0:T(8,128)(2,1)} %copy-done.6, bf16[512,768]{1,0:T(8,128)(2,1)} %copy-done.8, bf16[256,768]{1,0:T(8,128)(2,1)} %bitcast.20, ...), custom_call_target="tpu_custom_call" | custom-call | flops 3221225472 | bytes 14680064 | tf_op jit(solution)/shard_map/pallas_call | solution.py:152
  66.5 2.0 %collective-permute-start.6 = (f32[8,256]{1,0:T(8,128)}, f32[8,256]{1,0:T(8,128)S(1)}, u32[]{:S(2)}, u32[]{:S(2)}) collective-permute-start(f32[8,256]{1,0:T(8,128)} %get-tuple-element.18.row0), channel_id=1, source_target_pairs={{0,1},{1,0},{2,3},{3,2},{4,5},{5,4},{6,7},{7,6},{8,9},{9,8},{10,11... | collective-permute-start | bytes 24584 | tf_op jit(solution)/shard_map/ppermute | solution.py:44
  68.5 1.6 collective-permute-start.8
  71.9 2.1 %collective-permute-done.9.col1 = f32[8,256]{1,0:T(8,128)S(1)} collective-permute-done((f32[8,256]{1,0:T(8,128)}, f32[8,256]{1,0:T(8,128)S(1)}, u32[]{:S(2)}, u32[]{:S(2)}) %collective-permute-start.9) | collective-permute-done | bytes 8224 | tf_op jit(solution)/shard_map/ppermute | solution.py:44
  74.6 14.3 %shard_map.69 = (f32[256,768]{1,0:T(8,128)}, f32[256,768]{1,0:T(8,128)}, f32[256,768]{1,0:T(8,128)}, f32[256,768]{1,0:T(8,128)}, f32[2048,128]{1,0:T(8,128)}, /*index=5*/f32[8,256]{1,0:T(8,128)}, f32[8,128]{1,0:T(8,128)}) custom-call(f32[4]{0:T(128)} %pad_maximum_fusion.scal_ref, f32[4,2048,256]{2,1,0:T(8,128)} %get-tuple-element.17.s_ref, ...), custom_call_target="tpu_custom_call" | custom-call | flops 6442450944 | bytes 16777216 | tf_op jit(solution)/shard_map/pallas_call | solution.py:256
  89.0 14.1 %shard_map.70 = (f32[512,768]{1,0:T(8,128)}, f32[512,768]{1,0:T(8,128)}, f32[512,768]{1,0:T(8,128)}, f32[512,768]{1,0:T(8,128)}) custom-call(f32[4,2048,256]{2,1,0:T(8,128)} %get-tuple-element.17.s_ref, f32[2048,128]{1,0:T(8,128)} %get-tuple-element.21.r_ref, f32[8,256]{1,0:T(8,128)} %get-tuple-element.22.c_ref, bf16[256,768]{1,0:T(8,128)(2,1)} %bitcast.21, ...), custom_call_target="tpu_custom_call" | custom-call | flops 6442450944 | bytes 16777216 | tf_op jit(solution)/shard_map/pallas_call | solution.py:306
  103.1 2.7 %collective-permute-start.25 = (f32[512,768]{1,0:T(8,128)}, f32[512,768]{1,0:T(8,128)S(1)}, u32[]{:S(2)}, u32[]{:S(2)}) collective-permute-start(f32[512,768]{1,0:T(8,128)} %get-tuple-element.26), channel_id=1, source_target_pairs={{0,1},{1,0},{2,3},{3,2},{4,5},{5,4},{6,7},{7,6},{8,9},{9,8},{10,11... | collective-permute-start | bytes 4718600 | tf_op jit(solution)/shard_map/ppermute | solution.py:44
  106.5 2.1 %collective-permute-start.29 = (f32[256,768]{1,0:T(8,128)S(1)}, f32[256,768]{1,0:T(8,128)S(1)}, u32[]{:S(2)}, u32[]{:S(2)}) collective-permute-start(f32[256,768]{1,0:T(8,128)S(1)} %copy-done.9), channel_id=1, source_target_pairs={{0,12},{1,13},{2,14},{3,15},{4,0},{5,1},{6,2},{7,3},{8,4},{9,5},{1... | collective-permute-start | bytes 2359304 | tf_op jit(solution)/shard_map/ppermute | solution.py:44
  109.2 2.8 %add.171 = f32[512,768]{1,0:T(8,128)} add(f32[512,768]{1,0:T(8,128)} %get-tuple-element.25, f32[512,768]{1,0:T(8,128)S(1)} %collective-permute-done.25) | non-fusion elementwise | flops 393216 | bytes 4718592 | tf_op jit(solution)/shard_map/add | solution.py:377
  112.1 30.9 %collective-permute-done.27 = f32[256,768]{1,0:T(8,128)S(1)} collective-permute-done((f32[256,768]{1,0:T(8,128)S(1)}, f32[256,768]{1,0:T(8,128)S(1)}, u32[]{:S(2)}, u32[]{:S(2)}) %collective-permute-start.27) | collective-permute-done | bytes 786464 | tf_op jit(solution)/shard_map/ppermute | solution.py:44
  144.5 9.7 %all-to-all-start.1 = ((f32[16,16,768]{2,1,0:T(8,128)}), f32[16,16,768]{2,1,0:T(8,128)S(1)}, u32[]{:S(2)}, u32[]{:S(2)}) async-start(f32[16,16,768]{2,1,0:T(8,128)} %bitcast.12), calls=%async_computation.1 | async-start | bytes 1572864 | tf_op jit(solution)/shard_map/all_to_all | solution.py:374
  154.1 1.5 collective-permute-start.12
  156.0 1.3 collective-permute-start.14
  159.4 3.4 %collective-permute-start.16 = (f32[8,128]{1,0:T(8,128)S(1)}, f32[8,128]{1,0:T(8,128)S(1)}, u32[]{:S(2)}, u32[]{:S(2)}) collective-permute-start(f32[8,128]{1,0:T(8,128)S(1)} %add_add_fusion.3), channel_id=1, source_target_pairs={{0,8},{1,9},{2,10},{3,11},{4,12},{5,13},{6,14},{7,15},{8,0},{9,1},... | collective-permute-start | bytes 12296 | tf_op jit(solution)/shard_map/ppermute | solution.py:44
  164.1 1.4 collective-permute-done.17
  165.5 1.6 collective-permute-start.18
  167.1 2.0 %collective-permute-start.19 = (f32[8,128]{1,0:T(8,128)S(1)}, f32[8,128]{1,0:T(8,128)S(1)}, u32[]{:S(2)}, u32[]{:S(2)}) collective-permute-start(f32[8,128]{1,0:T(8,128)S(1)} %add_add_fusion.2), channel_id=1, source_target_pairs={{0,32},{16,48},{32,0},{48,16},{64,96},{80,112},{96,64},{112,80},{1... | collective-permute-start | bytes 12296 | tf_op jit(solution)/shard_map/ppermute | solution.py:327
  169.0 1.7 collective-permute-start.20
  172.3 5.0 %collective-permute-start.21 = (f32[8,128]{1,0:T(8,128)S(1)}, f32[8,128]{1,0:T(8,128)S(1)}, u32[]{:S(2)}, u32[]{:S(2)}) collective-permute-start(f32[8,128]{1,0:T(8,128)S(1)} %add_add_fusion.1), channel_id=1, source_target_pairs={{0,64},{16,80},{32,96},{48,112},{64,128},{80,144},{96,160},{112,17... | collective-permute-start | bytes 12296 | tf_op jit(solution)/shard_map/ppermute | solution.py:327
  177.3 2.7 %collective-permute-start.22 = (f32[8,128]{1,0:T(8,128)S(1)}, f32[8,128]{1,0:T(8,128)S(1)}, u32[]{:S(2)}, u32[]{:S(2)}) collective-permute-start(f32[8,128]{1,0:T(8,128)S(1)} %add_add_fusion.1), channel_id=1, source_target_pairs={{0,128},{16,144},{32,160},{48,176},{64,192},{80,208},{96,224},{112... | collective-permute-start | bytes 12296 | tf_op jit(solution)/shard_map/ppermute | solution.py:327
  180.0 2.8 %collective-permute-start.23 = (f32[8,128]{1,0:T(8,128)S(1)}, f32[8,128]{1,0:T(8,128)S(1)}, u32[]{:S(2)}, u32[]{:S(2)}) collective-permute-start(f32[8,128]{1,0:T(8,128)S(1)} %add_add_fusion.1), channel_id=1, source_target_pairs={{0,192},{16,208},{32,224},{48,240},{64,0},{80,16},{96,32},{112,48}... | collective-permute-start | bytes 12296 | tf_op jit(solution)/shard_map/ppermute | solution.py:327
  182.8 3.6 %collective-permute-done.23 = f32[8,128]{1,0:T(8,128)S(1)} collective-permute-done((f32[8,128]{1,0:T(8,128)S(1)}, f32[8,128]{1,0:T(8,128)S(1)}, u32[]{:S(2)}, u32[]{:S(2)}) %collective-permute-start.23) | collective-permute-done | bytes 4128 | tf_op jit(solution)/shard_map/ppermute | solution.py:327
  186.9 3.3 %add_multiply_fusion = f32[512,768]{1,0:T(8,128)} fusion(f32[512,768]{1,0:T(8,128)} %collective-permute-done.26, f32[512,768]{1,0:T(8,128)S(1)} %copy-done, f32[512,768]{1,0:T(8,128)} %collective-permute-done.24), kind=kLoop, calls=%fused_computation | loop fusion | flops 1179648 | bytes 6291456 | tf_op jit(solution)/shard_map/mul | solution.py:378
  (113 shorter events, 21.0 us)
Async XLA Ops:
  0.6 20.1 %collective-permute-start.1 = (bf16[512,768]{1,0:T(8,128)(2,1)}, bf16[512,768]{1,0:T(8,128)(2,1)S(1)}, u32[]{:S(2)}, u32[]{:S(2)}) collective-permute-start(bf16[512,768]{1,0:T(8,128)(2,1)} %x0.3), channel_id=1, source_target_pairs={{0,2},{1,3},{2,0},{3,1},{4,6},{5,7},{6,4},{7,5},{8,10},{9,11},{10,... | collective-permute-start | bytes 2359304 | tf_op jit(solution)/shard_map/ppermute | solution.py:44
  2.9 36.7 %collective-permute-start = (bf16[512,768]{1,0:T(8,128)(2,1)}, bf16[512,768]{1,0:T(8,128)(2,1)S(1)}, u32[]{:S(2)}, u32[]{:S(2)}) collective-permute-start(bf16[512,768]{1,0:T(8,128)(2,1)} %x0.3), channel_id=1, source_target_pairs={{0,1},{1,0},{2,3},{3,2},{4,5},{5,4},{6,7},{7,6},{8,9},{9,8},{10,11... | collective-permute-start | bytes 2359304 | tf_op jit(solution)/shard_map/ppermute | solution.py:44
  4.1 23.7 %all-to-all-start = ((bf16[16,16,768]{2,1,0:T(8,128)(2,1)}), bf16[16,16,768]{2,1,0:T(8,128)(2,1)S(1)}, u32[]{:S(2)}, u32[]{:S(2)}) async-start(bf16[16,16,768]{2,1,0:T(8,128)(2,1)} %bitcast.16), calls=%async_computation | async-start | bytes 786432 | tf_op jit(solution)/shard_map/all_to_all | solution.py:341
  20.7 30.4 %collective-permute-start.2 = (bf16[512,768]{1,0:T(8,128)(2,1)S(1)}, bf16[512,768]{1,0:T(8,128)(2,1)S(1)}, u32[]{:S(2)}, u32[]{:S(2)}) collective-permute-start(bf16[512,768]{1,0:T(8,128)(2,1)S(1)} %collective-permute-done.1.x2), channel_id=1, source_target_pairs={{0,1},{1,0},{2,3},{3,2},{4,5},{5,4},{6,7},{7,6},{8,9},{9,8},{10,11... | collective-permute-start | bytes 2359304 | tf_op jit(solution)/shard_map/ppermute | solution.py:44
  27.7 11.9 %collective-permute-start.3 = (bf16[256,768]{1,0:T(8,128)(2,1)S(1)}, bf16[256,768]{1,0:T(8,128)(2,1)S(1)}, u32[]{:S(2)}, u32[]{:S(2)}) collective-permute-start(bf16[256,768]{1,0:T(8,128)(2,1)S(1)} %bitcast.17), channel_id=1, source_target_pairs={{0,12},{1,13},{2,14},{3,15},{4,0},{5,1},{6,2},{7,3},{8,4},{9,5},{1... | collective-permute-start | bytes 1179656 | tf_op jit(solution)/shard_map/ppermute | solution.py:44
  30.2 9.9 %collective-permute-start.4 = (bf16[256,768]{1,0:T(8,128)(2,1)S(1)}, bf16[256,768]{1,0:T(8,128)(2,1)S(1)}, u32[]{:S(2)}, u32[]{:S(2)}) collective-permute-start(bf16[256,768]{1,0:T(8,128)(2,1)S(1)} %bitcast.18), channel_id=1, source_target_pairs={{0,8},{1,9},{2,10},{3,11},{4,12},{5,13},{6,14},{7,15},{8,0},{9,1},... | collective-permute-start | bytes 1179656 | tf_op jit(solution)/shard_map/ppermute | solution.py:44
  30.7 20.4 %collective-permute-start.5 = (bf16[256,768]{1,0:T(8,128)(2,1)S(1)}, bf16[256,768]{1,0:T(8,128)(2,1)S(1)}, u32[]{:S(2)}, u32[]{:S(2)}) collective-permute-start(bf16[256,768]{1,0:T(8,128)(2,1)S(1)} %bitcast.19), channel_id=1, source_target_pairs={{0,4},{1,5},{2,6},{3,7},{4,8},{5,9},{6,10},{7,11},{8,12},{9,13},{1... | collective-permute-start | bytes 1179656 | tf_op jit(solution)/shard_map/ppermute | solution.py:44
  65.7 4.4 %collective-permute-start.10 = (f32[8,256]{1,0:T(8,128)}, f32[8,256]{1,0:T(8,128)S(1)}, u32[]{:S(2)}, u32[]{:S(2)}) collective-permute-start(f32[8,256]{1,0:T(8,128)} %get-tuple-element.19.col0), channel_id=1, source_target_pairs={{0,8},{1,9},{2,10},{3,11},{4,12},{5,13},{6,14},{7,15},{8,0},{9,1},... | collective-permute-start | bytes 24584 | tf_op jit(solution)/shard_map/ppermute | solution.py:44
  66.4 4.9 %collective-permute-start.11 = (f32[8,256]{1,0:T(8,128)}, f32[8,256]{1,0:T(8,128)S(1)}, u32[]{:S(2)}, u32[]{:S(2)}) collective-permute-start(f32[8,256]{1,0:T(8,128)} %get-tuple-element.19.col0), channel_id=1, source_target_pairs={{0,12},{1,13},{2,14},{3,15},{4,0},{5,1},{6,2},{7,3},{8,4},{9,5},{1... | collective-permute-start | bytes 24584 | tf_op jit(solution)/shard_map/ppermute | solution.py:44
  66.5 4.8 %collective-permute-start.6 = (f32[8,256]{1,0:T(8,128)}, f32[8,256]{1,0:T(8,128)S(1)}, u32[]{:S(2)}, u32[]{:S(2)}) collective-permute-start(f32[8,256]{1,0:T(8,128)} %get-tuple-element.18.row0), channel_id=1, source_target_pairs={{0,1},{1,0},{2,3},{3,2},{4,5},{5,4},{6,7},{7,6},{8,9},{9,8},{10,11... | collective-permute-start | bytes 24584 | tf_op jit(solution)/shard_map/ppermute | solution.py:44
  68.5 2.9 %collective-permute-start.7 = (f32[8,256]{1,0:T(8,128)}, f32[8,256]{1,0:T(8,128)S(1)}, u32[]{:S(2)}, u32[]{:S(2)}) collective-permute-start(f32[8,256]{1,0:T(8,128)} %get-tuple-element.18.row0), channel_id=1, source_target_pairs={{0,2},{1,3},{2,0},{3,1},{4,6},{5,7},{6,4},{7,5},{8,10},{9,11},{10,... | collective-permute-start | bytes 24584 | tf_op jit(solution)/shard_map/ppermute | solution.py:44
  68.5 3.5 %collective-permute-start.8 = (f32[8,256]{1,0:T(8,128)}, f32[8,256]{1,0:T(8,128)S(1)}, u32[]{:S(2)}, u32[]{:S(2)}) collective-permute-start(f32[8,256]{1,0:T(8,128)} %get-tuple-element.18.row0), channel_id=1, source_target_pairs={{0,3},{1,2},{2,1},{3,0},{4,7},{5,6},{6,5},{7,4},{8,11},{9,10},{10,... | collective-permute-start | bytes 24584 | tf_op jit(solution)/shard_map/ppermute | solution.py:44
  70.1 3.9 %collective-permute-start.9 = (f32[8,256]{1,0:T(8,128)}, f32[8,256]{1,0:T(8,128)S(1)}, u32[]{:S(2)}, u32[]{:S(2)}) collective-permute-start(f32[8,256]{1,0:T(8,128)} %get-tuple-element.19.col0), channel_id=1, source_target_pairs={{0,4},{1,5},{2,6},{3,7},{4,8},{5,9},{6,10},{7,11},{8,12},{9,13},{1... | collective-permute-start | bytes 24584 | tf_op jit(solution)/shard_map/ppermute | solution.py:44
  103.1 6.1 %collective-permute-start.25 = (f32[512,768]{1,0:T(8,128)}, f32[512,768]{1,0:T(8,128)S(1)}, u32[]{:S(2)}, u32[]{:S(2)}) collective-permute-start(f32[512,768]{1,0:T(8,128)} %get-tuple-element.26), channel_id=1, source_target_pairs={{0,1},{1,0},{2,3},{3,2},{4,5},{5,4},{6,7},{7,6},{8,9},{9,8},{10,11... | collective-permute-start | bytes 4718600 | tf_op jit(solution)/shard_map/ppermute | solution.py:44
  105.8 37.2 %collective-permute-start.27 = (f32[256,768]{1,0:T(8,128)S(1)}, f32[256,768]{1,0:T(8,128)S(1)}, u32[]{:S(2)}, u32[]{:S(2)}) collective-permute-start(f32[256,768]{1,0:T(8,128)S(1)} %copy-done.11), channel_id=1, source_target_pairs={{0,4},{1,5},{2,6},{3,7},{4,8},{5,9},{6,10},{7,11},{8,12},{9,13},{1... | collective-permute-start | bytes 2359304 | tf_op jit(solution)/shard_map/ppermute | solution.py:44
  105.8 37.2 %collective-permute-start.28 = (f32[256,768]{1,0:T(8,128)S(1)}, f32[256,768]{1,0:T(8,128)S(1)}, u32[]{:S(2)}, u32[]{:S(2)}) collective-permute-start(f32[256,768]{1,0:T(8,128)S(1)} %copy-done.10), channel_id=1, source_target_pairs={{0,8},{1,9},{2,10},{3,11},{4,12},{5,13},{6,14},{7,15},{8,0},{9,1},... | collective-permute-start | bytes 2359304 | tf_op jit(solution)/shard_map/ppermute | solution.py:44
  106.5 36.9 %collective-permute-start.29 = (f32[256,768]{1,0:T(8,128)S(1)}, f32[256,768]{1,0:T(8,128)S(1)}, u32[]{:S(2)}, u32[]{:S(2)}) collective-permute-start(f32[256,768]{1,0:T(8,128)S(1)} %copy-done.9), channel_id=1, source_target_pairs={{0,12},{1,13},{2,14},{3,15},{4,0},{5,1},{6,2},{7,3},{8,4},{9,5},{1... | collective-permute-start | bytes 2359304 | tf_op jit(solution)/shard_map/ppermute | solution.py:44
  108.6 78.3 %collective-permute-start.24 = (f32[512,768]{1,0:T(8,128)}, f32[512,768]{1,0:T(8,128)}, u32[]{:S(2)}, u32[]{:S(2)}) collective-permute-start(f32[512,768]{1,0:T(8,128)} %get-tuple-element.24), channel_id=1, source_target_pairs={{0,1},{1,0},{2,3},{3,2},{4,5},{5,4},{6,7},{7,6},{8,9},{9,8},{10,11... | collective-permute-start | bytes 4718600 | tf_op jit(solution)/shard_map/ppermute | solution.py:44
  112.1 74.8 %collective-permute-start.26 = (f32[512,768]{1,0:T(8,128)}, f32[512,768]{1,0:T(8,128)}, u32[]{:S(2)}, u32[]{:S(2)}) collective-permute-start(f32[512,768]{1,0:T(8,128)} %add.171), channel_id=1, source_target_pairs={{0,2},{1,3},{2,0},{3,1},{4,6},{5,7},{6,4},{7,5},{8,10},{9,11},{10,... | collective-permute-start | bytes 4718600 | tf_op jit(solution)/shard_map/ppermute | solution.py:44
  144.5 42.4 %all-to-all-start.1 = ((f32[16,16,768]{2,1,0:T(8,128)}), f32[16,16,768]{2,1,0:T(8,128)S(1)}, u32[]{:S(2)}, u32[]{:S(2)}) async-start(f32[16,16,768]{2,1,0:T(8,128)} %bitcast.12), calls=%async_computation.1 | async-start | bytes 1572864 | tf_op jit(solution)/shard_map/all_to_all | solution.py:374
  154.1 3.2 %collective-permute-start.12 = (f32[8,128]{1,0:T(8,128)S(1)}, f32[8,128]{1,0:T(8,128)S(1)}, u32[]{:S(2)}, u32[]{:S(2)}) collective-permute-start(f32[8,128]{1,0:T(8,128)S(1)} %copy-done.5), channel_id=1, source_target_pairs={{0,1},{1,0},{2,3},{3,2},{4,5},{5,4},{6,7},{7,6},{8,9},{9,8},{10,11... | collective-permute-start | bytes 12296 | tf_op jit(solution)/shard_map/ppermute | solution.py:44
  155.6 2.7 %collective-permute-start.13 = (f32[8,128]{1,0:T(8,128)S(1)}, f32[8,128]{1,0:T(8,128)S(1)}, u32[]{:S(2)}, u32[]{:S(2)}) collective-permute-start(f32[8,128]{1,0:T(8,128)S(1)} %copy-done.5), channel_id=1, source_target_pairs={{0,2},{1,3},{2,0},{3,1},{4,6},{5,7},{6,4},{7,5},{8,10},{9,11},{10,... | collective-permute-start | bytes 12296 | tf_op jit(solution)/shard_map/ppermute | solution.py:44
  156.0 3.4 %collective-permute-start.14 = (f32[8,128]{1,0:T(8,128)S(1)}, f32[8,128]{1,0:T(8,128)S(1)}, u32[]{:S(2)}, u32[]{:S(2)}) collective-permute-start(f32[8,128]{1,0:T(8,128)S(1)} %copy-done.5), channel_id=1, source_target_pairs={{0,3},{1,2},{2,1},{3,0},{4,7},{5,6},{6,5},{7,4},{8,11},{9,10},{10,... | collective-permute-start | bytes 12296 | tf_op jit(solution)/shard_map/ppermute | solution.py:44
  159.4 4.0 %collective-permute-start.15 = (f32[8,128]{1,0:T(8,128)S(1)}, f32[8,128]{1,0:T(8,128)S(1)}, u32[]{:S(2)}, u32[]{:S(2)}) collective-permute-start(f32[8,128]{1,0:T(8,128)S(1)} %add_add_fusion.3), channel_id=1, source_target_pairs={{0,4},{1,5},{2,6},{3,7},{4,8},{5,9},{6,10},{7,11},{8,12},{9,13},{1... | collective-permute-start | bytes 12296 | tf_op jit(solution)/shard_map/ppermute | solution.py:44
  159.4 4.7 %collective-permute-start.16 = (f32[8,128]{1,0:T(8,128)S(1)}, f32[8,128]{1,0:T(8,128)S(1)}, u32[]{:S(2)}, u32[]{:S(2)}) collective-permute-start(f32[8,128]{1,0:T(8,128)S(1)} %add_add_fusion.3), channel_id=1, source_target_pairs={{0,8},{1,9},{2,10},{3,11},{4,12},{5,13},{6,14},{7,15},{8,0},{9,1},... | collective-permute-start | bytes 12296 | tf_op jit(solution)/shard_map/ppermute | solution.py:44
  162.7 2.8 %collective-permute-start.17 = (f32[8,128]{1,0:T(8,128)S(1)}, f32[8,128]{1,0:T(8,128)S(1)}, u32[]{:S(2)}, u32[]{:S(2)}) collective-permute-start(f32[8,128]{1,0:T(8,128)S(1)} %add_add_fusion.3), channel_id=1, source_target_pairs={{0,12},{1,13},{2,14},{3,15},{4,0},{5,1},{6,2},{7,3},{8,4},{9,5},{1... | collective-permute-start | bytes 12296 | tf_op jit(solution)/shard_map/ppermute | solution.py:44
  165.5 5.2 %collective-permute-start.18 = (f32[8,128]{1,0:T(8,128)S(1)}, f32[8,128]{1,0:T(8,128)S(1)}, u32[]{:S(2)}, u32[]{:S(2)}) collective-permute-start(f32[8,128]{1,0:T(8,128)S(1)} %add_add_fusion.2), channel_id=1, source_target_pairs={{0,16},{16,32},{32,48},{48,0},{64,80},{80,96},{96,112},{112,64},{1... | collective-permute-start | bytes 12296 | tf_op jit(solution)/shard_map/ppermute | solution.py:327
  167.1 4.6 %collective-permute-start.19 = (f32[8,128]{1,0:T(8,128)S(1)}, f32[8,128]{1,0:T(8,128)S(1)}, u32[]{:S(2)}, u32[]{:S(2)}) collective-permute-start(f32[8,128]{1,0:T(8,128)S(1)} %add_add_fusion.2), channel_id=1, source_target_pairs={{0,32},{16,48},{32,0},{48,16},{64,96},{80,112},{96,64},{112,80},{1... | collective-permute-start | bytes 12296 | tf_op jit(solution)/shard_map/ppermute | solution.py:327
  169.0 3.3 %collective-permute-start.20 = (f32[8,128]{1,0:T(8,128)S(1)}, f32[8,128]{1,0:T(8,128)S(1)}, u32[]{:S(2)}, u32[]{:S(2)}) collective-permute-start(f32[8,128]{1,0:T(8,128)S(1)} %add_add_fusion.2), channel_id=1, source_target_pairs={{0,48},{16,0},{32,16},{48,32},{64,112},{80,64},{96,80},{112,96},{1... | collective-permute-start | bytes 12296 | tf_op jit(solution)/shard_map/ppermute | solution.py:327
  172.3 10.4 %collective-permute-start.21 = (f32[8,128]{1,0:T(8,128)S(1)}, f32[8,128]{1,0:T(8,128)S(1)}, u32[]{:S(2)}, u32[]{:S(2)}) collective-permute-start(f32[8,128]{1,0:T(8,128)S(1)} %add_add_fusion.1), channel_id=1, source_target_pairs={{0,64},{16,80},{32,96},{48,112},{64,128},{80,144},{96,160},{112,17... | collective-permute-start | bytes 12296 | tf_op jit(solution)/shard_map/ppermute | solution.py:327
  177.3 5.5 %collective-permute-start.22 = (f32[8,128]{1,0:T(8,128)S(1)}, f32[8,128]{1,0:T(8,128)S(1)}, u32[]{:S(2)}, u32[]{:S(2)}) collective-permute-start(f32[8,128]{1,0:T(8,128)S(1)} %add_add_fusion.1), channel_id=1, source_target_pairs={{0,128},{16,144},{32,160},{48,176},{64,192},{80,208},{96,224},{112... | collective-permute-start | bytes 12296 | tf_op jit(solution)/shard_map/ppermute | solution.py:327
  180.0 6.4 %collective-permute-start.23 = (f32[8,128]{1,0:T(8,128)S(1)}, f32[8,128]{1,0:T(8,128)S(1)}, u32[]{:S(2)}, u32[]{:S(2)}) collective-permute-start(f32[8,128]{1,0:T(8,128)S(1)} %add_add_fusion.1), channel_id=1, source_target_pairs={{0,192},{16,208},{32,224},{48,240},{64,0},{80,16},{96,32},{112,48}... | collective-permute-start | bytes 12296 | tf_op jit(solution)/shard_map/ppermute | solution.py:327
  (21 other events, 287.0 us)
